TPU v7x, 512 devices: a whole 4x8x8 slice. The times are simulated.
512 devices in a mesh: tm: 32 (over z, y_lo), series: 16 (over x, y_hi, core).
Axes of the slice: x: 4, y: 8 (y_hi: 2, y_lo: 4; y = y_hi * 4 + y_lo), z: 8, core: 2. Of those that a mesh axis runs over, the one named last changes fastest.
Arguments:
- series_factors: bfloat16 [16384, 256], P(('series', 'tm')), may hold values from -1.5 to 1.5
- time_factors: bfloat16 [16384, 256], P(('tm', 'series')), may hold values from -1.5 to 1.5
- tile_values: bfloat16 [4096, 256, 256], P(('tm', 'series')), may hold values from -6 to 6
- tile_blocks: int32 [4096, 2], P(('tm', 'series')), may hold values from 0 to 63, as said below
- tile_counts: int32 [512], P(('tm', 'series')), may hold values from 1 to 8, as said below
- lags: int32 [96], replicated, may hold values from 1 to 168, as said below
- lag_weights: float32 [96, 256], replicated, may hold values from -0.4 to 0.4
Outputs:
- grad_series: float32 [16384, 256], P(('series', 'tm'))
- grad_time: float32 [16384, 256], P(('tm', 'series'))
Inputs may be any that keep to these rules, and one draw needn't show every extreme that they name: `tile_blocks`: row r names a series block in [4 s, 4 (s + 1)) and a time block in [2 t, 2 (t + 1)), where r // 8 = 16 t + s. `tile_counts`: at least one group lists 8 blocks. `lags`: Distinct, rising, and include 1 and 168.
All inputs are finite; a program needn't handle non-finite values.
Results may differ from a plain program's by a relative error of at most 0.0025.
Values may be sent and summed in bfloat16 or wider, within the bound.
A program may use at most 64 MiB of HBM per device.

v0:
```python
import jax
import jax.numpy as jnp
from jax import lax
from jax.sharding import PartitionSpec as P

LMAX = 168


def from_behind(x, axis, by):
    count = lax.axis_size(axis)
    pairs = [(i, i + by) for i in range(count) if 0 <= i + by < count]
    return lax.ppermute(x, axis, pairs)


def for_sending(x):
    return jax.tree.map(lambda a: a.astype(jnp.bfloat16) if a.dtype == jnp.float32 else a, x)


def depthwise(signal, kernel):
    return lax.conv_general_dilated(
        signal[None],
        kernel[:, None, :],
        (1,),
        "VALID",
        dimension_numbers=("NWC", "WIO", "NWC"),
        feature_group_count=signal.shape[1],
        precision=lax.Precision.HIGHEST,
    )[0]


def shards(series_factors, time_factors, tile_values, tile_blocks, tile_counts, lags, lag_weights):
    slab_index = lax.axis_index("tm")
    block_index = lax.axis_index("series")
    tile = tile_values.shape[1]
    rank = series_factors.shape[1]
    slots = tile_values.shape[0]
    f_block = lax.all_gather(series_factors, "tm", axis=0, tiled=True)
    x_slab = lax.all_gather(time_factors, "series", axis=0, tiled=True)
    block_rows = f_block.shape[0]
    slab_rows = x_slab.shape[0]
    series_count = block_rows // tile
    time_count = slab_rows // tile
    local_series = tile_blocks[:, 0] - block_index * series_count
    local_time = tile_blocks[:, 1] - slab_index * time_count
    used = tile_counts[0]
    valid = jnp.arange(slots) < used
    f_tiles = f_block.reshape(series_count, tile, rank)[local_series]
    x_tiles = x_slab.reshape(time_count, tile, rank)[local_time]
    pred = jnp.einsum("mak,mbk->mab", f_tiles, x_tiles, preferred_element_type=jnp.float32)
    resid = jnp.where(valid[:, None, None], tile_values.astype(jnp.float32) - pred, 0.0).astype(
        jnp.bfloat16
    )
    part_f = jnp.einsum("mab,mbk->mak", resid, x_tiles, preferred_element_type=jnp.float32)
    part_x = jnp.einsum("mab,mak->mbk", resid, f_tiles, preferred_element_type=jnp.float32)
    pick_series = (local_series[:, None] == jnp.arange(series_count)[None, :]).astype(jnp.float32)
    pick_time = (local_time[:, None] == jnp.arange(time_count)[None, :]).astype(jnp.float32)
    data_series = jnp.einsum(
        "ms,mak->sak", pick_series, part_f, precision=lax.Precision.HIGHEST
    ).reshape(block_rows, rank) * (-1.0 / tile)
    data_time = jnp.einsum(
        "ms,mak->sak", pick_time, part_x, precision=lax.Precision.HIGHEST
    ).reshape(slab_rows, rank) * (-1.0 / tile)
    own_series = series_factors.shape[0]
    summed = lax.psum(data_series, "tm")
    share_series = lax.dynamic_slice_in_dim(summed, slab_index * own_series, own_series, 0)
    grad_series = share_series + 0.5 * series_factors.astype(jnp.float32)
    before = from_behind(x_slab[slab_rows - LMAX :], "tm", 1)
    extended = jnp.concatenate([before, x_slab], axis=0).astype(jnp.float32)
    width = LMAX + 1
    place_past = (jnp.arange(width)[None, :] == (LMAX - lags)[:, None]).astype(jnp.float32)
    kernel_past = jnp.dot(place_past.T, lag_weights, precision=lax.Precision.HIGHEST)
    pred_ar = depthwise(extended, kernel_past)
    factors = x_slab.astype(jnp.float32)
    position = slab_index * slab_rows + jnp.arange(slab_rows)[:, None]
    err = jnp.where(position >= LMAX, factors - pred_ar, 0.0)
    after = from_behind(for_sending(err[:LMAX]), "tm", -1)
    err_ext = jnp.concatenate([err, after], axis=0)
    own_steps = time_factors.shape[0]
    own_start = block_index * own_steps
    window = lax.dynamic_slice_in_dim(err_ext, own_start, own_steps + LMAX, 0)
    place_future = (jnp.arange(width)[None, :] == lags[:, None]).astype(jnp.float32)
    kernel_future = jnp.dot(place_future.T, lag_weights, precision=lax.Precision.HIGHEST)
    ahead = depthwise(window, kernel_future)
    own_err = lax.dynamic_slice_in_dim(err, own_start, own_steps, 0)
    ar_grad = own_err - ahead
    share_time = lax.psum_scatter(data_time, "series", scatter_dimension=0, tiled=True)
    grad_time = share_time + 0.5 * time_factors.astype(jnp.float32) + 2.0 * ar_grad
    return (grad_series, grad_time)


def solution(mesh):
    placed = (
        P(("series", "tm"), None),
        P(("tm", "series"), None),
        P(("tm", "series"), None, None),
        P(("tm", "series"), None),
        P(("tm", "series")),
        P(),
        P(),
    )
    return jax.shard_map(
        shards,
        mesh=mesh,
        in_specs=placed,
        out_specs=(P(("series", "tm"), None), P(("tm", "series"), None)),
        check_vma=False,
    )
```

profile of v0, /device:TPU:6, one launch (start us, length us, event | category | flops | bytes accessed | tf_op | source)
XLA Modules:
  0.0 457.4 jit_solution(2669290870951678584)
XLA Ops:
  8.1 29.9 %all_gather.7 = bf16[512,256]{1,0:T(8,128)(2,1)S(1)} all-gather(bf16[32,256]{1,0:T(8,128)(2,1)} %param.8), channel_id=1, replica_groups=mesh['tm'=32,'series'=16] {'series'}, dimensions={0}, use_global_device_ids=true | all-gather | bytes 278528 | tf_op jit(solution)/shard_map/all_gather | solution.py:38
  38.0 87.0 %all_gather.6 = bf16[1024,256]{1,0:T(8,128)(2,1)S(1)} all-gather(bf16[32,256]{1,0:T(8,128)(2,1)} %param.7), channel_id=1, replica_groups=mesh['tm'=32,'series'=16] {'tm'}, dimensions={0}, use_global_device_ids=true | all-gather | bytes 540672 | tf_op jit(solution)/shard_map/all_gather | solution.py:37
  125.7 0.8 fusion.31
  126.5 0.6 gather_fusion.1
  127.1 0.6 gather_fusion
  127.7 1.7 select_convert_fusion
  129.5 0.5 fusion.33
  130.0 0.5 copy-done.1
  130.4 2.2 fusion.7
  132.7 0.8 copy.12
  133.6 1.3 collective-permute-start
  134.9 0.4 fusion.32
  135.4 2.2 fusion.4
  137.6 1.2 copy.11
  138.9 0.4 convolution_bitcast_fusion.1
  139.3 13.2 %fusion.10 = f32[1,512,256]{2,0,1:T(1,128)S(1)} fusion(bf16[1,680,256]{2,1,0:T(8,128)(2,1)S(1)} %maximum_bitcast_fusion, f32[169,1,256]{2,0,1:T(8,128)S(1)} %convolution_bitcast_fusion.1), kind=kOutput, calls=%fused_computation.13 | convolution fusion | flops 265814016 | bytes 1045504 | tf_op jit(solution)/shard_map/conv_general_dilated | solution.py:20
  152.7 1.3 collective-permute-start.1
  154.0 0.4 convolution_bitcast_fusion
  154.4 4.9 %collective-permute-done.1 = bf16[168,256]{1,0:T(8,128)(2,1)S(1)} collective-permute-done((bf16[168,256]{1,0:T(8,128)(2,1)S(1)}, bf16[168,256]{1,0:T(8,128)(2,1)S(1)}, u32[]{:S(2)}, u32[]{:S(2)}) %collective-permute-start.1) | collective-permute-done | bytes 86048 | tf_op jit(solution)/shard_map/ppermute | solution.py:12
  159.5 0.6 fusion.14
  160.1 50.1 %reduce-scatter.2.cloned.1.call-done = f32[32,256]{1,0:T(8,128)} async-done(((f32[512,256]{1,0:T(8,128)}), f32[32,256]{1,0:T(8,128)}) %reduce-scatter.2.cloned.1.call-update) | async-done | bytes 32784 | tf_op jit(solution)/shard_map/reduce_scatter | solution.py:86
  210.3 1.4 fusion.20
  211.7 237.0 %all-reduce.2.cloned.1.call-done = f32[1024,256]{1,0:T(8,128)} async-done(((f32[1024,256]{1,0:T(8,128)}), f32[1024,256]{1,0:T(8,128)}) %all-reduce.2.cloned.1.call-update) | async-done | bytes 1048592 | tf_op jit(solution)/shard_map/psum | solution.py:64
  448.6 1.4 multiply_add_fusion
  (27 shorter events, 0.6 us)
Async XLA Ops:
  8.0 130.9 %copy-start = (f32[96,256]{1,0:T(8,128)S(1)}, f32[96,256]{1,0:T(8,128)}, u32[]{:S(2)}) copy-start(f32[96,256]{1,0:T(8,128)} %param.13) | copy-start | bytes 294916
  8.0 202.3 %reduce-scatter.2.cloned.1.call-start = ((), (), s32[]{:S(2)}) async-start(), calls=%async_computation.2 | async-start | bytes 557056 | tf_op jit(solution)/shard_map/reduce_scatter | solution.py:86
  129.4 1.0 copy-start.1
  132.7 2.3 copy-start.2
  133.5 315.1 %all-reduce.2.cloned.1.call-start = ((), (), s32[]{:S(2)}) async-start(), calls=%async_computation.1 | async-start | bytes 2097152 | tf_op jit(solution)/shard_map/psum | solution.py:64
  133.6 5.6 %collective-permute-start = (bf16[168,256]{1,0:T(8,128)(2,1)S(1)}, bf16[168,256]{1,0:T(8,128)(2,1)S(1)}, u32[]{:S(2)}, u32[]{:S(2)}) collective-permute-start(bf16[168,256]{1,0:T(8,128)(2,1)S(1)} %slice.21), channel_id=1, source_target_pairs={{0,16},{16,32},{32,48},{48,64},{64,80},{80,96},{96,112},{112,128},... | collective-permute-start | bytes 258056 | tf_op jit(solution)/shard_map/ppermute | solution.py:12
  137.6 1.2 copy-start.5
  152.7 6.6 %collective-permute-start.1 = (bf16[168,256]{1,0:T(8,128)(2,1)S(1)}, bf16[168,256]{1,0:T(8,128)(2,1)S(1)}, u32[]{:S(2)}, u32[]{:S(2)}) collective-permute-start(bf16[168,256]{1,0:T(8,128)(2,1)S(1)} %slice.34), channel_id=1, source_target_pairs={{16,0},{32,16},{48,32},{64,48},{80,64},{96,80},{112,96},{128,112},... | collective-permute-start | bytes 258056 | tf_op jit(solution)/shard_map/ppermute | solution.py:12
  159.5 50.8 %copy-start.3 = (bf16[32,256]{1,0:T(8,128)(2,1)S(1)}, bf16[32,256]{1,0:T(8,128)(2,1)}, u32[]{:S(2)}) copy-start(bf16[32,256]{1,0:T(8,128)(2,1)} %param.8) | copy-start | bytes 49156
  159.5 289.1 %copy-start.4 = (bf16[32,256]{1,0:T(8,128)(2,1)S(1)}, bf16[32,256]{1,0:T(8,128)(2,1)}, u32[]{:S(2)}) copy-start(bf16[32,256]{1,0:T(8,128)(2,1)} %param.7) | copy-start | bytes 49156
Sparse Core Ops, SparseCore 0:
  133.7 76.5 reduce-scatter.1
Sparse Core Ops, SparseCore 1:
  138.9 309.6 all-reduce.1
where the time goes:
time: 458 us; the launch traced here: 457 us
  waiting for transfers between devices  292 us (64%)
  blocking collectives  117 us (26%)
  matrix products  21.7 us (5%)
  between operations  16.4 us (4%)
    psum x1, waiting for transfers between devices, shards(): summed = lax.psum(data_series, 'tm')  237 us
    all_gather x1, blocking collectives, shards(): f_block = lax.all_gather(series_factors, 'tm', axis=0, tiled=True)  87 us
    reduce_scatter x1, waiting for transfers between devices, shards(): lax.psum_scatter(data_time, 'series', scatter_dimension=0, tiled=True)  50.1 us
    all_gather x1, blocking collectives, shards(): x_slab = lax.all_gather(time_factors, 'series', axis=0, tiled=True)  29.9 us
    conv_general_dilated x2, matrix products, depthwise(): lax.conv_general_dilated(signal[None], kernel[:, None, :], (1,), 'VALID',...  13.8 us
  transfers between devices with their start and end apart: 4, of which 3 were waited for; matrix products, arithmetic and copies ran while one was open for 4% of the time, Pallas kernels for 0%

commit v1 on v0

v1 whole, which is shorter than its diff:
```python
import jax
import jax.numpy as jnp
from jax import lax
from jax.experimental import pallas as pl
from jax.experimental.pallas import tpu as pltpu
from jax.sharding import PartitionSpec as P

LMAX = 168
NZ, NY, NX, NH, NC = 8, 4, 4, 2, 2
ROWS = 32
TILE = 256
HALF = 128
SB = NZ * NY * ROWS // TILE
TB = NX * NH * NC * ROWS // TILE
SLAB = NX * NH * NC
HALO = 6
ERR = ROWS + LMAX
MESH = pl.DeviceIdType.MESH
F32 = jnp.float32
BF16 = jnp.bfloat16


def contract(a, b, da, db):
    return lax.dot_general(a, b, (((da,), (db,)), ((), ())), preferred_element_type=F32)


def kernel(
    sf, tf, values, blocks, counts, lags, weights, out_s, out_t,
    tv, fa, fb, xw, before, after, acc_s, acc_t, pa, pb, pt, za, yb, qa, qb, ya, zb,
    rc, qc, rx, qx, rh, wf, eb, ww, local_sem,
    fa_y, fa_z, fb_z, fb_y, x_h, x_x, x_c, halo, sa_z, sa_y, sb_y, sb_z, t_c, t_x, t_h,
):
    tm, s = lax.axis_index("tm"), lax.axis_index("series")
    z, y = tm // NY, tm % NY
    x, h, c = s // (NH * NC), (s // NC) % NH, s % NC

    def at_z(i):
        return (i * NY + y, s)

    def at_y(i):
        return (z * NY + i, s)

    def at_x(i):
        return (tm, i * (NH * NC) + h * NC + c)

    other_h = (tm, x * (NH * NC) + (1 - h) * NC + c)
    other_c = (tm, x * (NH * NC) + h * NC + (1 - c))

    load_values = pltpu.make_async_copy(values, tv, local_sem)
    load_values.start()

    takes_past = (s < HALO) & (tm > 0)
    gives_past = (s < HALO) & (tm < NZ * NY - 1)
    takes_next = (s >= SLAB - HALO) & (tm < NZ * NY - 1)
    gives_next = (s >= SLAB - HALO) & (tm > 0)

    barrier = pltpu.get_barrier_semaphore()

    def greet(device):
        pl.semaphore_signal(barrier, inc=1, device_id=device, device_id_type=MESH)

    for d in range(1, NY):
        greet(at_y((y + d) % NY))
    for d in range(1, NZ):
        greet(at_z((z + d) % NZ))
    for d in range(1, NX):
        greet(at_x((x + d) % NX))
    greet(other_h)
    greet(other_c)

    @pl.when(takes_past)
    def _():
        greet((tm - 1, s))

    @pl.when(takes_next)
    def _():
        greet((tm + 1, s))

    fa[z, y] = sf[:, :HALF]
    fb[z, y] = sf[:, HALF:]
    xw[s] = tf[...]
    more = jnp.where(gives_past | gives_next, 1, 0)
    pl.semaphore_wait(barrier, NY - 1 + NZ - 1 + NX - 1 + 2 + more)

    sent = []

    def copy(src, dst, sems, i, device):
        return pltpu.make_async_remote_copy(
            src_ref=src, dst_ref=dst, send_sem=sems.at[0, i], recv_sem=sems.at[1, i],
            device_id=device, device_id_type=MESH,
        )

    def send(src, dst, sems, i, device):
        one = copy(src, dst, sems, i, device)
        one.start()
        sent.append(one)

    def arrive(dst, sems, i, device):
        copy(dst, dst, sems, i, device).wait_recv()

    send(xw.at[s], xw.at[s], x_h, 0, other_h)
    for d in range(1, NY):
        send(fa.at[z, y], fa.at[z, y], fa_y, d - 1, at_y((y + d) % NY))
    for d in range(1, NZ):
        send(fb.at[z, y], fb.at[z, y], fb_z, d - 1, at_z((z + d) % NZ))

    def slab_block(i, j, k):
        return i * (NH * NC) + j * NC + k

    arrive(xw.at[slab_block(x, 1 - h, c)], x_h, 0, other_h)
    for d in range(1, NX):
        for j in range(NH):
            part = xw.at[slab_block(x, j, c)]
            send(part, part, x_x, (d - 1) * NH + j, at_x((x + d) % NX))

    for d in range(1, NY):
        arrive(fa.at[z, (y + NY - d) % NY], fa_y, d - 1, at_y((y + d) % NY))
    for d in range(1, NZ):
        send(fa.at[z], fa.at[z], fa_z, d - 1, at_z((z + d) % NZ))
    for d in range(1, NZ):
        arrive(fb.at[(z + NZ - d) % NZ, y], fb_z, d - 1, at_z((z + d) % NZ))
    for d in range(1, NY):
        send(fb.at[:, y], fb.at[:, y], fb_y, d - 1, at_y((y + d) % NY))

    for d in range(1, NX):
        for j in range(NH):
            got = xw.at[slab_block((x + NX - d) % NX, j, c)]
            arrive(got, x_x, (d - 1) * NH + j, at_x((x + d) % NX))
    for i in range(NX):
        for j in range(NH):
            part = xw.at[slab_block(i, j, c)]
            send(part, part, x_c, i * NH + j, other_c)
    for i in range(NX):
        for j in range(NH):
            arrive(xw.at[slab_block(i, j, 1 - c)], x_c, i * NH + j, other_c)

    give_past = copy(xw.at[pl.ds(SLAB - HALO, HALO)], before, halo, 0, (tm + 1, s))
    give_next = copy(xw.at[pl.ds(0, HALO)], after, halo, 1, (tm - 1, s))
    take_past = copy(before, before, halo, 0, (tm - 1, s))
    take_next = copy(after, after, halo, 1, (tm + 1, s))

    @pl.when(gives_past)
    def _():
        give_past.start()

    @pl.when(gives_next)
    def _():
        give_next.start()

    acc_s[...] = jnp.zeros_like(acc_s)
    acc_t[...] = jnp.zeros_like(acc_t)
    ww[0] = weights[:, :HALF]
    ww[1] = weights[:, HALF:]

    load_values.wait()
    for d in range(1, NZ):
        arrive(fa.at[(z + NZ - d) % NZ], fa_z, d - 1, at_z((z + d) % NZ))
    for d in range(1, NY):
        arrive(fb.at[:, (y + NY - d) % NY], fb_y, d - 1, at_y((y + d) % NY))

    used = counts[0]
    per_z = TILE // (NY * ROWS)
    per_x = TILE // ROWS

    def slot(m, carry):
        at_series = lax.rem(blocks[m, 0], SB)
        at_time = lax.rem(blocks[m, 1], TB)
        f_left = fa[pl.ds(at_series * per_z, per_z)].reshape(TILE, HALF)
        f_right = fb[pl.ds(at_series * per_z, per_z)].reshape(TILE, HALF)
        f = jnp.concatenate([f_left, f_right], axis=1)
        t = xw[pl.ds(at_time * per_x, per_x)].reshape(TILE, TILE)
        pred = contract(f, t, 1, 1)
        resid = jnp.where(m < used, tv[m].astype(F32) - pred, 0.0).astype(BF16)
        part_s = contract(resid, t, 1, 0)
        part_t = contract(resid, f, 0, 0)
        for k in range(SB):
            acc_s[k] += jnp.where(at_series == k, part_s, 0.0)
        for k in range(TB):
            acc_t[k] += jnp.where(at_time == k, part_t, 0.0)
        return carry

    lax.fori_loop(0, values.shape[0], slot, 0)

    scale = -1.0 / TILE
    for k in range(TB):
        part = (acc_t[k] * scale).astype(BF16).reshape(per_x, ROWS, TILE)
        pt[pl.ds(k * per_x, per_x)] = part
    for i in range(NX):
        for j in range(NH):
            n = i * NH + j
            send(pt.at[n * NC + (1 - c)], rc.at[n], t_c, n, other_c)
    for k in range(SB):
        part = (acc_s[k] * scale).astype(BF16).reshape(per_z, NY, ROWS, TILE)
        pa[pl.ds(k * per_z, per_z)] = part[..., :HALF]
        pb[pl.ds(k * per_z, per_z)] = part[..., HALF:]
    for d in range(1, NZ):
        there = (z + d) % NZ
        send(pa.at[there], za.at[d - 1], sa_z, d - 1, at_z(there))
    for d in range(1, NY):
        there = (y + d) % NY
        send(pb.at[:, there], yb.at[d - 1], sb_y, d - 1, at_y(there))

    def widen(rows, first):
        rows = rows.astype(F32).reshape(-1, TILE)
        wf[0, pl.ds(first * ROWS, rows.shape[0])] = rows[:, :HALF]
        wf[1, pl.ds(first * ROWS, rows.shape[0])] = rows[:, HALF:]

    nothing = jnp.zeros((HALO, ROWS, TILE), BF16)
    widen(xw[...], HALO)

    @pl.when(takes_past)
    def _():
        take_past.wait_recv()
        widen(before[...], 0)

    @pl.when(jnp.logical_not(takes_past))
    def _():
        widen(nothing, 0)

    @pl.when(takes_next)
    def _():
        take_next.wait_recv()
        widen(after[...], HALO + SLAB)

    @pl.when(jnp.logical_not(takes_next))
    def _():
        widen(nothing, HALO + SLAB)

    steps = tm * (SLAB * ROWS) + s * ROWS + lax.broadcasted_iota(jnp.int32, (ERR, HALF), 0)
    inside = (steps >= LMAX) & (steps < NZ * NY * SLAB * ROWS)

    base = (HALO + s) * ROWS

    def errors(side):
        def add(m, total):
            w = ww[side, pl.ds(m, 1), :]
            return total + w * wf[side, pl.ds(base - lags[m], ERR), :]

        pred = lax.fori_loop(0, lags.shape[0], add, jnp.zeros((ERR, HALF), F32))
        eb[side] = jnp.where(inside, wf[side, pl.ds(pl.multiple_of(base, ROWS), ERR), :] - pred, 0.0)

    def ahead(side):
        def add(m, total):
            w = ww[side, pl.ds(m, 1), :]
            return total + w * eb[side, pl.ds(lags[m], ROWS), :]

        return lax.fori_loop(0, lags.shape[0], add, jnp.zeros((ROWS, HALF), F32))

    errors(0)

    for n in range(NX * NH):
        arrive(rc.at[n], t_c, n, other_c)
    for n in range(NX * NH):
        qc[n] = pt[n * NC + c].astype(F32) + rc[n].astype(F32)
    for d in range(1, NX):
        there = (x + d) % NX
        send(qc.at[pl.ds(there * NH, NH)], rx.at[d - 1], t_x, d - 1, at_x(there))

    errors(1)

    for d in range(1, NX):
        arrive(rx.at[d - 1], t_x, d - 1, at_x((x + d) % NX))
    qx[...] = qc[pl.ds(x * NH, NH)] + rx[0] + rx[1] + rx[2]
    send(qx.at[1 - h], rh, t_h, 0, other_h)

    for d in range(1, NY):
        arrive(yb.at[d - 1], sb_y, d - 1, at_y((y + d) % NY))
    total = pb[:, y].astype(F32)
    for d in range(1, NY):
        total = total + yb[d - 1].astype(F32)
    qb[...] = total
    for d in range(1, NZ):
        there = (z + d) % NZ
        send(qb.at[there], zb.at[d - 1], sb_z, d - 1, at_z(there))
    for d in range(1, NZ):
        arrive(za.at[d - 1], sa_z, d - 1, at_z((z + d) % NZ))
    total = pa[z].astype(F32)
    for d in range(1, NZ):
        total = total + za[d - 1].astype(F32)
    qa[...] = total
    for d in range(1, NY):
        there = (y + d) % NY
        send(qa.at[there], ya.at[d - 1], sa_y, d - 1, at_y(there))

    grads = [2.0 * (eb[side, pl.ds(0, ROWS), :] - ahead(side)) for side in range(2)]
    arrive(rh, t_h, 0, other_h)
    own = qx[h] + rh[...] + 0.5 * tf[...].astype(F32)
    out_t[...] = own + jnp.concatenate(grads, axis=1)

    for d in range(1, NZ):
        arrive(zb.at[d - 1], sb_z, d - 1, at_z((z + d) % NZ))
    right = qb[z]
    for d in range(1, NZ):
        right = right + zb[d - 1]
    for d in range(1, NY):
        arrive(ya.at[d - 1], sa_y, d - 1, at_y((y + d) % NY))
    left = qa[y]
    for d in range(1, NY):
        left = left + ya[d - 1]
    out_s[...] = jnp.concatenate([left, right], axis=1) + 0.5 * sf[...].astype(F32)

    for one in sent:
        one.wait_send()

    @pl.when(gives_past)
    def _():
        give_past.wait_send()

    @pl.when(gives_next)
    def _():
        give_next.wait_send()


def shards(series_factors, time_factors, tile_values, tile_blocks, tile_counts, lags, lag_weights):
    vmem = pl.BlockSpec(memory_space=pltpu.VMEM)
    smem = pl.BlockSpec(memory_space=pltpu.SMEM)
    slots = tile_values.shape[0]
    own = jax.ShapeDtypeStruct((ROWS, TILE), F32)

    def pair(n):
        return pltpu.SemaphoreType.DMA((2, n))

    return tuple(
        pl.pallas_call(
            kernel,
            out_shape=(own, own),
            in_specs=[vmem, vmem, pl.BlockSpec(memory_space=pl.ANY), smem, smem, smem, vmem],
            out_specs=(vmem, vmem),
            scratch_shapes=[
                pltpu.VMEM((slots, TILE, TILE), BF16),
                pltpu.VMEM((NZ, NY, ROWS, HALF), BF16),
                pltpu.VMEM((NZ, NY, ROWS, HALF), BF16),
                pltpu.VMEM((SLAB, ROWS, TILE), BF16),
                pltpu.VMEM((HALO, ROWS, TILE), BF16),
                pltpu.VMEM((HALO, ROWS, TILE), BF16),
                pltpu.VMEM((SB, TILE, TILE), F32),
                pltpu.VMEM((TB, TILE, TILE), F32),
                pltpu.VMEM((NZ, NY, ROWS, HALF), BF16),
                pltpu.VMEM((NZ, NY, ROWS, HALF), BF16),
                pltpu.VMEM((SLAB, ROWS, TILE), BF16),
                pltpu.VMEM((NZ - 1, NY, ROWS, HALF), BF16),
                pltpu.VMEM((NY - 1, NZ, ROWS, HALF), BF16),
                pltpu.VMEM((NY, ROWS, HALF), F32),
                pltpu.VMEM((NZ, ROWS, HALF), F32),
                pltpu.VMEM((NY - 1, ROWS, HALF), F32),
                pltpu.VMEM((NZ - 1, ROWS, HALF), F32),
                pltpu.VMEM((NX * NH, ROWS, TILE), BF16),
                pltpu.VMEM((NX * NH, ROWS, TILE), F32),
                pltpu.VMEM((NX - 1, NH, ROWS, TILE), F32),
                pltpu.VMEM((NH, ROWS, TILE), F32),
                pltpu.VMEM((ROWS, TILE), F32),
                pltpu.VMEM((2, (SLAB + 2 * HALO) * ROWS, HALF), F32),
                pltpu.VMEM((2, ERR, HALF), F32),
                pltpu.VMEM((2, *lags.shape, HALF), F32),
                pltpu.SemaphoreType.DMA,
                pair(NY - 1), pair(NZ - 1), pair(NZ - 1), pair(NY - 1),
                pair(1), pair((NX - 1) * NH), pair(NX * NH), pair(2),
                pair(NZ - 1), pair(NY - 1), pair(NY - 1), pair(NZ - 1),
                pair(NX * NH), pair(NX - 1), pair(1),
            ],
            compiler_params=pltpu.CompilerParams(
                collective_id=0, has_side_effects=True, vmem_limit_bytes=40 * 2**20
            ),
            cost_estimate=pl.CostEstimate(
                flops=slots * 6 * TILE**3, bytes_accessed=slots * 2 * TILE**2, transcendentals=0
            ),
        )(series_factors, time_factors, tile_values, tile_blocks, tile_counts, lags, lag_weights)
    )


def solution(mesh):
    placed = (
        P(("series", "tm"), None),
        P(("tm", "series"), None),
        P(("tm", "series"), None, None),
        P(("tm", "series"), None),
        P(("tm", "series")),
        P(),
        P(),
    )
    return jax.shard_map(
        shards,
        mesh=mesh,
        in_specs=placed,
        out_specs=(P(("series", "tm"), None), P(("tm", "series"), None)),
        check_vma=False,
    )
```

time: 458 us -> 51.5 us (0.11)
  the two profiles are of different devices: /device:TPU:6 before, /device:TPU:1 now
where the time goes in v1:
time: 51.5 us; the launch traced here: 51 us
  Pallas kernels  44.2 us (86%)
  local copies, waits for them, and re-layouts  5.44 us (11%)
  between operations  1.32 us (3%)
    pallas_call x1, Pallas kernels, shards(): pl.pallas_call(kernel, out_shape=(own, own), in_specs=[vmem, vmem, pl.Blo...  44.2 us
    unnamed x15, local copies, waits for them, and re-layouts  5.44 us

profile of v1, /device:TPU:1, one launch (start us, length us, event | category | flops | bytes accessed | tf_op | source)
XLA Modules:
  0.0 51.0 jit_solution(4670911268897138834)
XLA Ops:
  0.6 0.0 copy-start.5
  1.3 0.0 copy-done.5
  1.3 0.0 copy-start.4
  1.3 0.1 copy.9.blocks
  1.4 0.6 %copy-done.4 = s32[96]{0:T(128)S(1)} copy-done((s32[96]{0:T(128)S(1)}, s32[96]{0:T(128)}, u32[]{:S(2)}) %copy-start.4) | copy-done | bytes 408
  2.0 0.0 copy-start
  2.0 1.2 %copy-done = bf16[8,256,256]{2,1,0:T(8,128)(2,1)S(1)} copy-done((bf16[8,256,256]{2,1,0:T(8,128)(2,1)S(1)}, bf16[8,256,256]{2,1,0:T(8,128)(2,1)}, u32[]{:S(2)}) %copy-start) | copy-done | bytes 1048600
  3.2 0.0 copy-start.1
  3.2 0.9 %copy-done.1 = f32[96,256]{1,0:T(8,128)S(1)} copy-done((f32[96,256]{1,0:T(8,128)S(1)}, f32[96,256]{1,0:T(8,128)}, u32[]{:S(2)}) %copy-start.1) | copy-done | bytes 98328
  4.1 0.0 copy-start.2
  4.1 0.7 %copy-done.2 = bf16[32,256]{1,0:T(8,128)(2,1)S(1)} copy-done((bf16[32,256]{1,0:T(8,128)(2,1)S(1)}, bf16[32,256]{1,0:T(8,128)(2,1)}, u32[]{:S(2)}) %copy-start.2) | copy-done | bytes 16408
  4.8 0.0 copy-start.3
  4.8 0.7 %copy-done.3 = bf16[32,256]{1,0:T(8,128)(2,1)S(1)} copy-done((bf16[32,256]{1,0:T(8,128)(2,1)S(1)}, bf16[32,256]{1,0:T(8,128)(2,1)}, u32[]{:S(2)}) %copy-start.3) | copy-done | bytes 16408
  5.5 44.2 %shard_map.86 = (f32[32,256]{1,0:T(8,128)S(1)}, f32[32,256]{1,0:T(8,128)S(1)}) custom-call(bf16[32,256]{1,0:T(8,128)(2,1)S(1)} %copy-done.2, bf16[32,256]{1,0:T(8,128)(2,1)S(1)} %copy-done.3, bf16[8,256,256]{2,1,0:T(8,128)(2,1)S(1)} %copy-done, s32[8,2]{1,0:T(8,128)S(1)} %copy.9.blocks, s32[1]{0:T(128)S(6)} %copy.12.counts, s32[96]{0:T(128)S(1)} %copy-done.4, ...), custom_call_target="tpu_custom_call" | custom-call | flops 805306368 | bytes 1048576 | tf_op jit(solution)/shard_map/pallas_call | solution.py:324
  49.8 0.6 %copy.13 = f32[32,256]{1,0:T(8,128)} copy(f32[32,256]{1,0:T(8,128)S(1)} %get-tuple-element.4) | data formatting | bytes 65536
  50.4 0.6 %copy.14 = f32[32,256]{1,0:T(8,128)} copy(f32[32,256]{1,0:T(8,128)S(1)} %get-tuple-element.5) | data formatting | bytes 65536
Async XLA Ops:
  0.6 0.7 %copy-start.5 = (s32[8,2]{0,1:T(2,128)S(1)}, s32[8,2]{0,1:T(2,128)}, u32[]{:S(2)}) copy-start(s32[8,2]{0,1:T(2,128)} %param.10) | copy-start | bytes 196
  1.3 0.7 %copy-start.4 = (s32[96]{0:T(128)S(1)}, s32[96]{0:T(128)}, u32[]{:S(2)}) copy-start(s32[96]{0:T(128)} %lags.1) | copy-start | bytes 1156
  2.0 1.2 %copy-start = (bf16[8,256,256]{2,1,0:T(8,128)(2,1)S(1)}, bf16[8,256,256]{2,1,0:T(8,128)(2,1)}, u32[]{:S(2)}) copy-start(bf16[8,256,256]{2,1,0:T(8,128)(2,1)} %values.1) | copy-start | bytes 3145732
  3.2 0.9 %copy-start.1 = (f32[96,256]{1,0:T(8,128)S(1)}, f32[96,256]{1,0:T(8,128)}, u32[]{:S(2)}) copy-start(f32[96,256]{1,0:T(8,128)} %weights.1) | copy-start | bytes 294916
  4.1 0.7 %copy-start.2 = (bf16[32,256]{1,0:T(8,128)(2,1)S(1)}, bf16[32,256]{1,0:T(8,128)(2,1)}, u32[]{:S(2)}) copy-start(bf16[32,256]{1,0:T(8,128)(2,1)} %sf.1) | copy-start | bytes 49156
  4.8 0.7 %copy-start.3 = (bf16[32,256]{1,0:T(8,128)(2,1)S(1)}, bf16[32,256]{1,0:T(8,128)(2,1)}, u32[]{:S(2)}) copy-start(bf16[32,256]{1,0:T(8,128)(2,1)} %tf.1) | copy-start | bytes 49156

commit v2 on v1

v2 whole, which is shorter than its diff:
```python
import jax
import jax.numpy as jnp
from jax import lax
from jax.experimental import pallas as pl
from jax.experimental.pallas import tpu as pltpu
from jax.sharding import PartitionSpec as P

LMAX = 168
NZ, NY, NX, NH, NC = 8, 4, 4, 2, 2
ROWS = 32
TILE = 256
HALF = 128
SB = NZ * NY * ROWS // TILE
TB = NX * NH * NC * ROWS // TILE
SLAB = NX * NH * NC
NEAR = [(i, j) for i in range(NX) for j in range(NC) if i + j]
HALO = 6
ERR = ROWS + LMAX
MESH = pl.DeviceIdType.MESH
F32 = jnp.float32
BF16 = jnp.bfloat16


def contract(a, b, da, db):
    return lax.dot_general(a, b, (((da,), (db,)), ((), ())), preferred_element_type=F32)


def kernel(
    sf_in, tf_in, values, blocks_in, counts_in, lags_in, weights_in, out,
    sf, tf, blocks, counts, lags, weights, tv, fa, fb, xw, before, after, acc_s, acc_t, pa, pb, pt, za, yb, qa, qb, ya, zb,
    rx, qx, rh, wf, eb, ww, local_sem,
    fa_y, fa_z, fb_z, fb_y, x_h, x_x, halo, sa_z, sa_y, sb_y, sb_z, t_x, t_h,
):
    tm, s = lax.axis_index("tm"), lax.axis_index("series")
    z, y = tm // NY, tm % NY
    x, h, c = s // (NH * NC), s // NC % NH, s % NC
    s_far = s + NC * (1 - 2 * h)

    def at_z(i):
        return (i * NY + y, s)

    def at_y(i):
        return (z * NY + i, s)

    def near(i, j):
        return (x + i) % NX * NH, (c + j) % NC

    def at_near(i, j):
        row, core = near(i, j)
        return (tm, (row + h) * NC + core)

    def from_near(i, j):
        return near(NX - i, NC - j)

    takes_past = (s < HALO) & (tm > 0)
    gives_past = (s < HALO) & (tm < NZ * NY - 1)
    takes_next = (s >= SLAB - HALO) & (tm < NZ * NY - 1)
    gives_next = (s >= SLAB - HALO) & (tm > 0)

    barrier = pltpu.get_barrier_semaphore()

    def greet(device):
        pl.semaphore_signal(barrier, inc=1, device_id=device, device_id_type=MESH)

    for d in range(1, NY):
        greet(at_y((y + d) % NY))
    for d in range(1, NZ):
        greet(at_z((z + d) % NZ))
    for i, j in NEAR:
        greet(at_near(i, j))
    greet((tm, s_far))

    @pl.when(takes_past)
    def _():
        greet((tm - 1, s))

    @pl.when(takes_next)
    def _():
        greet((tm + 1, s))

    loads = [
        pltpu.make_async_copy(src, dst, local_sem.at[i])
        for i, (src, dst) in enumerate(
            [(tf_in, tf), (sf_in, sf), (values, tv), (weights_in, weights), (lags_in, lags), (blocks_in, blocks), (counts_in, counts)]
        )
    ]
    for one in loads:
        one.start()

    loads[0].wait()
    loads[1].wait()
    fa[z, y] = sf[:, :HALF]
    fb[z, y] = sf[:, HALF:]
    xw[x * NH + h, c] = tf[...]
    more = jnp.where(gives_past | gives_next, 1, 0)
    pl.semaphore_wait(barrier, NY - 1 + NZ - 1 + len(NEAR) + 1 + more)

    sent = []

    def copy(src, dst, sems, i, device):
        return pltpu.make_async_remote_copy(
            src_ref=src, dst_ref=dst, send_sem=sems.at[0, i], recv_sem=sems.at[1, i],
            device_id=device, device_id_type=MESH,
        )

    def send(src, dst, sems, i, device):
        one = copy(src, dst, sems, i, device)
        one.start()
        sent.append(one)

    def arrive(dst, sems, i, device):
        copy(dst, dst, sems, i, device).wait_recv()

    send(xw.at[x * NH + h, c], xw.at[x * NH + h, c], x_h, 0, (tm, s_far))
    for d in range(1, NY):
        send(fa.at[z, y], fa.at[z, y], fa_y, d - 1, at_y((y + d) % NY))
    for d in range(1, NZ):
        send(fb.at[z, y], fb.at[z, y], fb_z, d - 1, at_z((z + d) % NZ))

    for d in range(1, NY):
        arrive(fa.at[z, (y + NY - d) % NY], fa_y, d - 1, at_y((y + d) % NY))
    for d in range(1, NZ):
        send(fa.at[z], fa.at[z], fa_z, d - 1, at_z((z + d) % NZ))
    for d in range(1, NZ):
        arrive(fb.at[(z + NZ - d) % NZ, y], fb_z, d - 1, at_z((z + d) % NZ))
    for d in range(1, NY):
        send(fb.at[:, y], fb.at[:, y], fb_y, d - 1, at_y((y + d) % NY))

    arrive(xw.at[x * NH + 1 - h, c], x_h, 0, (tm, s_far))
    part = xw.at[pl.ds(x * NH, NH), c]
    for n, (i, j) in enumerate(NEAR):
        send(part, part, x_x, n, at_near(i, j))
    for one in loads[2:]:
        one.wait()
    ww[0] = weights[:, :HALF]
    ww[1] = weights[:, HALF:]
    for n, (i, j) in enumerate(NEAR):
        row, core = from_near(i, j)
        arrive(xw.at[pl.ds(row, NH), core], x_x, n, at_near(i, j))
    give_past = copy(xw.at[pl.ds(SLAB // NC - HALO // NC, HALO // NC)], before, halo, 0, (tm + 1, s))
    give_next = copy(xw.at[pl.ds(0, HALO // NC)], after, halo, 1, (tm - 1, s))
    take_past = copy(before, before, halo, 0, (tm - 1, s))
    take_next = copy(after, after, halo, 1, (tm + 1, s))

    @pl.when(gives_past)
    def _():
        give_past.start()

    @pl.when(gives_next)
    def _():
        give_next.start()

    for d in range(1, NZ):
        arrive(fa.at[(z + NZ - d) % NZ], fa_z, d - 1, at_z((z + d) % NZ))
    for d in range(1, NY):
        arrive(fb.at[:, (y + NY - d) % NY], fb_y, d - 1, at_y((y + d) % NY))

    used = counts[0]
    per_z = TILE // (NY * ROWS)
    per_x = TILE // ROWS

    series_of, time_of = [], []
    for m in range(values.shape[0]):
        at_series = lax.rem(blocks[0, m], SB)
        at_time = lax.rem(blocks[1, m], TB)
        series_of.append(at_series)
        time_of.append(at_time)
        f_left = fa[pl.ds(at_series * per_z, per_z)].reshape(TILE, HALF)
        f_right = fb[pl.ds(at_series * per_z, per_z)].reshape(TILE, HALF)
        f = jnp.concatenate([f_left, f_right], axis=1)
        t = xw[pl.ds(at_time * (per_x // NC), per_x // NC)].reshape(TILE, TILE)
        pred = contract(f, t, 1, 1)
        resid = jnp.where(m < used, tv[m].astype(F32) - pred, 0.0).astype(BF16)
        acc_s[m] = contract(resid, t, 1, 0)
        acc_t[m] = contract(resid, f, 0, 0)

    scale = -1.0 / TILE
    rows_at_once = 64

    def gathered(acc, places, k, piece):
        total = jnp.zeros((rows_at_once, TILE), F32)
        for m, place in enumerate(places):
            total = total + jnp.where(place == k, acc[m, pl.ds(pl.multiple_of(piece * rows_at_once, rows_at_once), rows_at_once)], 0.0)
        return (total * scale).astype(BF16)

    def pack_time(piece, carry):
        for k in range(TB):
            part = gathered(acc_t, time_of, k, piece).reshape(-1, NC, ROWS, TILE)
            pt[pl.ds(k * (per_x // NC) + piece * part.shape[0], part.shape[0])] = part
        return carry

    lax.fori_loop(0, TILE // rows_at_once, pack_time, 0)
    for n, (i, j) in enumerate(NEAR):
        row, core = near(i, j)
        send(pt.at[pl.ds(row, NH), core], rx.at[n], t_x, n, at_near(i, j))

    def pack_series(piece, carry):
        per = NY * ROWS // rows_at_once
        for k in range(SB):
            part = gathered(acc_s, series_of, k, piece).reshape(-1, ROWS, TILE)
            there = (k * per_z + piece // per, pl.ds(piece % per * part.shape[0], part.shape[0]))
            pa[there] = part[..., :HALF]
            pb[there] = part[..., HALF:]
        return carry

    lax.fori_loop(0, TILE // rows_at_once, pack_series, 0)
    for d in range(1, NZ):
        there = (z + d) % NZ
        send(pa.at[there], za.at[d - 1], sa_z, d - 1, at_z(there))
    for d in range(1, NY):
        there = (y + d) % NY
        send(pb.at[:, there], yb.at[d - 1], sb_y, d - 1, at_y(there))

    def widen(rows, first):
        rows = rows.astype(F32).reshape(-1, TILE)
        wf[0, pl.ds(first * ROWS, rows.shape[0])] = rows[:, :HALF]
        wf[1, pl.ds(first * ROWS, rows.shape[0])] = rows[:, HALF:]

    nothing = jnp.zeros((HALO // NC, NC, ROWS, TILE), BF16)
    widen(xw[...], HALO)

    @pl.when(takes_past)
    def _():
        take_past.wait_recv()
        widen(before[...], 0)

    @pl.when(jnp.logical_not(takes_past))
    def _():
        widen(nothing, 0)

    @pl.when(takes_next)
    def _():
        take_next.wait_recv()
        widen(after[...], HALO + SLAB)

    @pl.when(jnp.logical_not(takes_next))
    def _():
        widen(nothing, HALO + SLAB)

    steps = tm * (SLAB * ROWS) + s * ROWS + lax.broadcasted_iota(jnp.int32, (ERR, HALF), 0)
    inside = (steps >= LMAX) & (steps < NZ * NY * SLAB * ROWS)

    base = (HALO + s) * ROWS

    def errors(side):
        def add(m, total):
            w = ww[side, pl.ds(m, 1), :]
            return total + w * wf[side, pl.ds(base - lags[m], ERR), :]

        pred = lax.fori_loop(0, lags.shape[0], add, jnp.zeros((ERR, HALF), F32))
        eb[side] = jnp.where(inside, wf[side, pl.ds(pl.multiple_of(base, ROWS), ERR), :] - pred, 0.0)

    def ahead(side):
        def add(m, total):
            w = ww[side, pl.ds(m, 1), :]
            return total + w * eb[side, pl.ds(lags[m], ROWS), :]

        return lax.fori_loop(0, lags.shape[0], add, jnp.zeros((ROWS, HALF), F32))

    errors(0)

    for n, (i, j) in enumerate(NEAR):
        arrive(rx.at[n], t_x, n, at_near(i, j))
    total = pt[pl.ds(x * NH, NH), c].astype(F32)
    for n in range(len(NEAR)):
        total = total + rx[n].astype(F32)
    qx[...] = total
    send(qx.at[1 - h], rh, t_h, 0, (tm, s_far))

    for d in range(1, NY):
        arrive(yb.at[d - 1], sb_y, d - 1, at_y((y + d) % NY))
    total = pb[:, y].astype(F32)
    for d in range(1, NY):
        total = total + yb[d - 1].astype(F32)
    qb[...] = total
    for d in range(1, NZ):
        there = (z + d) % NZ
        send(qb.at[there], zb.at[d - 1], sb_z, d - 1, at_z(there))
    for d in range(1, NZ):
        arrive(za.at[d - 1], sa_z, d - 1, at_z((z + d) % NZ))
    total = pa[z].astype(F32)
    for d in range(1, NZ):
        total = total + za[d - 1].astype(F32)
    qa[...] = total
    for d in range(1, NY):
        there = (y + d) % NY
        send(qa.at[there], ya.at[d - 1], sa_y, d - 1, at_y(there))

    errors(1)
    grads = [2.0 * (eb[side, pl.ds(0, ROWS), :] - ahead(side)) for side in range(2)]
    arrive(rh, t_h, 0, (tm, s_far))
    own = qx[h] + rh[...]
    out[1] = own + jnp.concatenate(grads, axis=1)

    for d in range(1, NZ):
        arrive(zb.at[d - 1], sb_z, d - 1, at_z((z + d) % NZ))
    right = qb[z]
    for d in range(1, NZ):
        right = right + zb[d - 1]
    for d in range(1, NY):
        arrive(ya.at[d - 1], sa_y, d - 1, at_y((y + d) % NY))
    left = qa[y]
    for d in range(1, NY):
        left = left + ya[d - 1]
    out[0] = jnp.concatenate([left, right], axis=1)

    for one in sent:
        one.wait_send()

    @pl.when(gives_past)
    def _():
        give_past.wait_send()

    @pl.when(gives_next)
    def _():
        give_next.wait_send()


def shards(series_factors, time_factors, tile_values, tile_blocks, tile_counts, lags, lag_weights):
    vmem = pl.BlockSpec(memory_space=pltpu.VMEM)
    anywhere = pl.BlockSpec(memory_space=pl.ANY)
    slots = tile_values.shape[0]
    own = jax.ShapeDtypeStruct((2, ROWS, TILE), F32)

    def pair(n):
        return pltpu.SemaphoreType.DMA((2, n))

    both = pl.pallas_call(
            kernel,
            out_shape=own,
            in_specs=[anywhere] * 7,
            out_specs=vmem,
            scratch_shapes=[
                pltpu.VMEM((ROWS, TILE), BF16),
                pltpu.VMEM((ROWS, TILE), BF16),
                pltpu.SMEM((2, slots), jnp.int32),
                pltpu.SMEM((1,), jnp.int32),
                pltpu.SMEM(lags.shape, jnp.int32),
                pltpu.VMEM(lag_weights.shape, F32),
                pltpu.VMEM((slots, TILE, TILE), BF16),
                pltpu.VMEM((NZ, NY, ROWS, HALF), BF16),
                pltpu.VMEM((NZ, NY, ROWS, HALF), BF16),
                pltpu.VMEM((SLAB // NC, NC, ROWS, TILE), BF16),
                pltpu.VMEM((HALO // NC, NC, ROWS, TILE), BF16),
                pltpu.VMEM((HALO // NC, NC, ROWS, TILE), BF16),
                pltpu.VMEM((slots, TILE, TILE), F32),
                pltpu.VMEM((slots, TILE, TILE), F32),
                pltpu.VMEM((NZ, NY, ROWS, HALF), BF16),
                pltpu.VMEM((NZ, NY, ROWS, HALF), BF16),
                pltpu.VMEM((SLAB // NC, NC, ROWS, TILE), BF16),
                pltpu.VMEM((NZ - 1, NY, ROWS, HALF), BF16),
                pltpu.VMEM((NY - 1, NZ, ROWS, HALF), BF16),
                pltpu.VMEM((NY, ROWS, HALF), F32),
                pltpu.VMEM((NZ, ROWS, HALF), F32),
                pltpu.VMEM((NY - 1, ROWS, HALF), F32),
                pltpu.VMEM((NZ - 1, ROWS, HALF), F32),
                pltpu.VMEM((len(NEAR), NH, ROWS, TILE), BF16),
                pltpu.VMEM((NH, ROWS, TILE), F32),
                pltpu.VMEM((ROWS, TILE), F32),
                pltpu.VMEM((2, (SLAB + 2 * HALO) * ROWS, HALF), F32),
                pltpu.VMEM((2, ERR, HALF), F32),
                pltpu.VMEM((2, *lags.shape, HALF), F32),
                pltpu.SemaphoreType.DMA((7,)),
                pair(NY - 1), pair(NZ - 1), pair(NZ - 1), pair(NY - 1),
                pair(1), pair(len(NEAR)), pair(2),
                pair(NZ - 1), pair(NY - 1), pair(NY - 1), pair(NZ - 1),
                pair(len(NEAR)), pair(1),
            ],
            compiler_params=pltpu.CompilerParams(
                collective_id=0, has_side_effects=True, vmem_limit_bytes=60 * 2**20
            ),
            cost_estimate=pl.CostEstimate(
                flops=slots * 6 * TILE**3, bytes_accessed=slots * 2 * TILE**2, transcendentals=0
            ),
        )(series_factors, time_factors, tile_values, tile_blocks.T, tile_counts, lags, lag_weights)
    return both[0] + 0.5 * series_factors.astype(F32), both[1] + 0.5 * time_factors.astype(F32)


def solution(mesh):
    placed = (
        P(("series", "tm"), None),
        P(("tm", "series"), None),
        P(("tm", "series"), None, None),
        P(("tm", "series"), None),
        P(("tm", "series")),
        P(),
        P(),
    )
    return jax.shard_map(
        shards,
        mesh=mesh,
        in_specs=placed,
        out_specs=(P(("series", "tm"), None), P(("tm", "series"), None)),
        check_vma=False,
    )
```

time: 51.5 us -> 44.7 us (0.87)
  the two profiles are of different devices: /device:TPU:1 before, /device:TPU:30 now
where the time goes in v2:
time: 44.7 us; the launch traced here: 44.5 us
  Pallas kernels  41.8 us (94%)
  other arithmetic  1.41 us (3%)
  between operations  1.32 us (3%)
    pallas_call x1, Pallas kernels, shards(): pl.pallas_call(kernel, out_shape=own, in_specs=[anywhere] * 7, out_specs=...  41.8 us
    add x1, other arithmetic, shards(): both[1] + 0.5 * time_factors.astype(F32)  1.41 us

profile of v2, /device:TPU:30, one launch (start us, length us, event | category | flops | bytes accessed | tf_op | source)
XLA Modules:
  0.0 44.5 jit_solution(180931609732575574)
XLA Ops:
  1.3 0.0 copy-start
  1.3 0.0 copy-start.1
  1.3 41.8 %shard_map.86 = f32[2,32,256]{2,1,0:T(8,128)} custom-call(bf16[32,256]{1,0:T(8,128)(2,1)} %sf_in.1, bf16[32,256]{1,0:T(8,128)(2,1)} %tf_in.1, bf16[8,256,256]{2,1,0:T(8,128)(2,1)} %values.1, s32[2,8]{1,0:T(2,128)} %bitcast.5, s32[1]{0:T(128)S(6)} %copy.9.counts_in, s32[96]{0:T(128)} %lags_in.1, f32[96,256]{1,0:T(8,128)} %weights_in.1), custom_call_target="tpu_custom_call" | custom-call | flops 805306368 | bytes 1048576 | tf_op jit(solution)/shard_map/pallas_call | solution.py:328
  43.1 0.0 copy-done
  43.1 0.0 copy-done.1
  43.1 1.4 %bitcast_add_fusion = (f32[32,256]{1,0:T(8,128)}, f32[32,256]{1,0:T(8,128)}) fusion(bf16[32,256]{1,0:T(8,128)(2,1)S(1)} %copy-done, f32[2,32,256]{2,1,0:T(8,128)} %shard_map.86, bf16[32,256]{1,0:T(8,128)(2,1)S(1)} %copy-done.1), kind=kLoop, calls=%fused_computation | loop fusion | flops 49152 | bytes 163840 | tf_op jit(solution)/shard_map/add | solution.py:376
Async XLA Ops:
  1.3 41.8 %copy-start = (bf16[32,256]{1,0:T(8,128)(2,1)S(1)}, bf16[32,256]{1,0:T(8,128)(2,1)}, u32[]{:S(2)}) copy-start(bf16[32,256]{1,0:T(8,128)(2,1)} %tf_in.1) | copy-start | bytes 49156
  1.3 41.8 %copy-start.1 = (bf16[32,256]{1,0:T(8,128)(2,1)S(1)}, bf16[32,256]{1,0:T(8,128)(2,1)}, u32[]{:S(2)}) copy-start(bf16[32,256]{1,0:T(8,128)(2,1)} %sf_in.1) | copy-start | bytes 49156

commit v3 on v2

--- a/solution.py
+++ b/solution.py
@@ -13,6 +13,7 @@
 SB = NZ * NY * ROWS // TILE
 TB = NX * NH * NC * ROWS // TILE
 SLAB = NX * NH * NC
+SHIFTS = (2, 1, 3, 0)
 NEAR = [(i, j) for i in range(NX) for j in range(NC) if i + j]
 HALO = 6
 ERR = ROWS + LMAX
@@ -27,7 +28,7 @@
 
 def kernel(
     sf_in, tf_in, values, blocks_in, counts_in, lags_in, weights_in, out,
-    sf, tf, blocks, counts, lags, weights, tv, fa, fb, xw, before, after, acc_s, acc_t, pa, pb, pt, za, yb, qa, qb, ya, zb,
+    sf, tf, blocks, counts, lags, weights, left_over, tv, fa, fb, xw, before, after, acc_s, acc_t, pa, pb, pt, za, yb, qa, qb, ya, zb, qb16,
     rx, qx, rh, wf, eb, ww, local_sem,
     fa_y, fa_z, fb_z, fb_y, x_h, x_x, halo, sa_z, sa_y, sb_y, sb_z, t_x, t_h,
 ):
@@ -98,8 +99,9 @@
     sent = []
 
     def copy(src, dst, sems, i, device):
+        i = i if isinstance(i, tuple) else (i, i)
         return pltpu.make_async_remote_copy(
-            src_ref=src, dst_ref=dst, send_sem=sems.at[0, i], recv_sem=sems.at[1, i],
+            src_ref=src, dst_ref=dst, send_sem=sems.at[0, i[0]], recv_sem=sems.at[1, i[1]],
             device_id=device, device_id_type=MESH,
         )
 
@@ -159,20 +161,23 @@
     per_z = TILE // (NY * ROWS)
     per_x = TILE // ROWS
 
+    def factor_rows(at):
+        left = fa[pl.ds(at * per_z, per_z)].reshape(TILE, HALF)
+        right = fb[pl.ds(at * per_z, per_z)].reshape(TILE, HALF)
+        return jnp.concatenate([left, right], axis=1)
+
     series_of, time_of = [], []
     for m in range(values.shape[0]):
         at_series = lax.rem(blocks[0, m], SB)
         at_time = lax.rem(blocks[1, m], TB)
         series_of.append(at_series)
         time_of.append(at_time)
-        f_left = fa[pl.ds(at_series * per_z, per_z)].reshape(TILE, HALF)
-        f_right = fb[pl.ds(at_series * per_z, per_z)].reshape(TILE, HALF)
-        f = jnp.concatenate([f_left, f_right], axis=1)
+        f = factor_rows(at_series)
         t = xw[pl.ds(at_time * (per_x // NC), per_x // NC)].reshape(TILE, TILE)
         pred = contract(f, t, 1, 1)
         resid = jnp.where(m < used, tv[m].astype(F32) - pred, 0.0).astype(BF16)
+        left_over[m] = resid
         acc_s[m] = contract(resid, t, 1, 0)
-        acc_t[m] = contract(resid, f, 0, 0)
 
     scale = -1.0 / TILE
     rows_at_once = 64
@@ -183,6 +188,32 @@
             total = total + jnp.where(place == k, acc[m, pl.ds(pl.multiple_of(piece * rows_at_once, rows_at_once), rows_at_once)], 0.0)
         return (total * scale).astype(BF16)
 
+    per = NY * ROWS // rows_at_once
+    own_block = z // per_z
+
+    def pack_series(k):
+        def one(piece, carry):
+            part = gathered(acc_s, series_of, k, piece).reshape(-1, ROWS, TILE)
+            there = (k * per_z + piece // per, pl.ds(piece % per * part.shape[0], part.shape[0]))
+            pa[there] = part[..., :HALF]
+            pb[there] = part[..., HALF:]
+            return carry
+
+        lax.fori_loop(0, TILE // rows_at_once, one, 0)
+
+    for n, shift in enumerate(SHIFTS):
+        k = (own_block + shift) % SB
+        pack_series(k)
+        for e in range(per_z if shift else 1):
+            there = k * per_z + e if shift else own_block * per_z + (z + 1) % per_z
+            send(pa.at[there], za.at[z], sa_z, (n * per_z + e, z), at_z(there))
+    for d in range(1, NY):
+        there = (y + d) % NY
+        send(pb.at[:, there], yb.at[d - 1], sb_y, d - 1, at_y(there))
+
+    for m in range(values.shape[0]):
+        acc_t[m] = contract(left_over[m], factor_rows(series_of[m]), 0, 0)
+
     def pack_time(piece, carry):
         for k in range(TB):
             part = gathered(acc_t, time_of, k, piece).reshape(-1, NC, ROWS, TILE)
@@ -193,23 +224,6 @@
     for n, (i, j) in enumerate(NEAR):
         row, core = near(i, j)
         send(pt.at[pl.ds(row, NH), core], rx.at[n], t_x, n, at_near(i, j))
-
-    def pack_series(piece, carry):
-        per = NY * ROWS // rows_at_once
-        for k in range(SB):
-            part = gathered(acc_s, series_of, k, piece).reshape(-1, ROWS, TILE)
-            there = (k * per_z + piece // per, pl.ds(piece % per * part.shape[0], part.shape[0]))
-            pa[there] = part[..., :HALF]
-            pb[there] = part[..., HALF:]
-        return carry
-
-    lax.fori_loop(0, TILE // rows_at_once, pack_series, 0)
-    for d in range(1, NZ):
-        there = (z + d) % NZ
-        send(pa.at[there], za.at[d - 1], sa_z, d - 1, at_z(there))
-    for d in range(1, NY):
-        there = (y + d) % NY
-        send(pb.at[:, there], yb.at[d - 1], sb_y, d - 1, at_y(there))
 
     def widen(rows, first):
         rows = rows.astype(F32).reshape(-1, TILE)
@@ -273,14 +287,17 @@
     for d in range(1, NY):
         total = total + yb[d - 1].astype(F32)
     qb[...] = total
+    qb16[...] = total.astype(BF16)
     for d in range(1, NZ):
         there = (z + d) % NZ
-        send(qb.at[there], zb.at[d - 1], sb_z, d - 1, at_z(there))
-    for d in range(1, NZ):
-        arrive(za.at[d - 1], sa_z, d - 1, at_z((z + d) % NZ))
+        send(qb16.at[there], zb.at[d - 1], sb_z, d - 1, at_z(there))
+    for n, shift in enumerate(SHIFTS):
+        for e in range(per_z if shift else 1):
+            source = (own_block + SB - shift) % SB * per_z + e if shift else own_block * per_z + (z + 1) % per_z
+            arrive(za.at[source], sa_z, (0, source), at_z(source))
     total = pa[z].astype(F32)
     for d in range(1, NZ):
-        total = total + za[d - 1].astype(F32)
+        total = total + za[(z + d) % NZ].astype(F32)
     qa[...] = total
     for d in range(1, NY):
         there = (y + d) % NY
@@ -296,7 +313,7 @@
         arrive(zb.at[d - 1], sb_z, d - 1, at_z((z + d) % NZ))
     right = qb[z]
     for d in range(1, NZ):
-        right = right + zb[d - 1]
+        right = right + zb[d - 1].astype(F32)
     for d in range(1, NY):
         arrive(ya.at[d - 1], sa_y, d - 1, at_y((y + d) % NY))
     left = qa[y]
@@ -338,6 +355,7 @@
                 pltpu.SMEM(lags.shape, jnp.int32),
                 pltpu.VMEM(lag_weights.shape, F32),
                 pltpu.VMEM((slots, TILE, TILE), BF16),
+                pltpu.VMEM((slots, TILE, TILE), BF16),
                 pltpu.VMEM((NZ, NY, ROWS, HALF), BF16),
                 pltpu.VMEM((NZ, NY, ROWS, HALF), BF16),
                 pltpu.VMEM((SLAB // NC, NC, ROWS, TILE), BF16),
@@ -348,12 +366,13 @@
                 pltpu.VMEM((NZ, NY, ROWS, HALF), BF16),
                 pltpu.VMEM((NZ, NY, ROWS, HALF), BF16),
                 pltpu.VMEM((SLAB // NC, NC, ROWS, TILE), BF16),
-                pltpu.VMEM((NZ - 1, NY, ROWS, HALF), BF16),
+                pltpu.VMEM((NZ, NY, ROWS, HALF), BF16),
                 pltpu.VMEM((NY - 1, NZ, ROWS, HALF), BF16),
                 pltpu.VMEM((NY, ROWS, HALF), F32),
                 pltpu.VMEM((NZ, ROWS, HALF), F32),
                 pltpu.VMEM((NY - 1, ROWS, HALF), F32),
-                pltpu.VMEM((NZ - 1, ROWS, HALF), F32),
+                pltpu.VMEM((NZ - 1, ROWS, HALF), BF16),
+                pltpu.VMEM((NZ, ROWS, HALF), BF16),
                 pltpu.VMEM((len(NEAR), NH, ROWS, TILE), BF16),
                 pltpu.VMEM((NH, ROWS, TILE), F32),
                 pltpu.VMEM((ROWS, TILE), F32),
@@ -363,7 +382,7 @@
                 pltpu.SemaphoreType.DMA((7,)),
                 pair(NY - 1), pair(NZ - 1), pair(NZ - 1), pair(NY - 1),
                 pair(1), pair(len(NEAR)), pair(2),
-                pair(NZ - 1), pair(NY - 1), pair(NY - 1), pair(NZ - 1),
+                pair(NZ), pair(NY - 1), pair((NY - 1) * SB), pair(NZ - 1),
                 pair(len(NEAR)), pair(1),
             ],
             compiler_params=pltpu.CompilerParams(

time: 44.7 us -> 43.3 us (0.969)
  the two profiles are of different devices: /device:TPU:30 before, /device:TPU:1 now
where the time goes in v3:
time: 43.3 us; the launch traced here: 43 us
  Pallas kernels  40.3 us (93%)
  other arithmetic  1.41 us (3%)
  between operations  1.32 us (3%)
    pallas_call x1, Pallas kernels, shards(): pl.pallas_call(kernel, out_shape=own, in_specs=[anywhere] * 7, out_specs=...  40.3 us
    add x1, other arithmetic, shards(): both[1] + 0.5 * time_factors.astype(F32)  1.41 us

profile of v3, /device:TPU:1, one launch (start us, length us, event | category | flops | bytes accessed | tf_op | source)
XLA Modules:
  0.0 43.0 jit_solution(10713958506201037047)
XLA Ops:
  1.3 0.0 copy-start
  1.3 0.0 copy-start.1
  1.3 40.3 %shard_map.86 = f32[2,32,256]{2,1,0:T(8,128)} custom-call(bf16[32,256]{1,0:T(8,128)(2,1)} %sf_in.1, bf16[32,256]{1,0:T(8,128)(2,1)} %tf_in.1, bf16[8,256,256]{2,1,0:T(8,128)(2,1)} %values.1, s32[2,8]{1,0:T(2,128)} %bitcast.5, s32[1]{0:T(128)S(6)} %copy.9.counts_in, s32[96]{0:T(128)} %lags_in.1, f32[96,256]{1,0:T(8,128)} %weights_in.1), custom_call_target="tpu_custom_call" | custom-call | flops 805306368 | bytes 1048576 | tf_op jit(solution)/shard_map/pallas_call | solution.py:345
  41.6 0.0 copy-done
  41.6 0.0 copy-done.1
  41.6 1.4 %bitcast_add_fusion = (f32[32,256]{1,0:T(8,128)}, f32[32,256]{1,0:T(8,128)}) fusion(bf16[32,256]{1,0:T(8,128)(2,1)S(1)} %copy-done, f32[2,32,256]{2,1,0:T(8,128)} %shard_map.86, bf16[32,256]{1,0:T(8,128)(2,1)S(1)} %copy-done.1), kind=kLoop, calls=%fused_computation | loop fusion | flops 49152 | bytes 163840 | tf_op jit(solution)/shard_map/add | solution.py:395
Async XLA Ops:
  1.3 40.3 %copy-start = (bf16[32,256]{1,0:T(8,128)(2,1)S(1)}, bf16[32,256]{1,0:T(8,128)(2,1)}, u32[]{:S(2)}) copy-start(bf16[32,256]{1,0:T(8,128)(2,1)} %tf_in.1) | copy-start | bytes 49156
  1.3 40.3 %copy-start.1 = (bf16[32,256]{1,0:T(8,128)(2,1)S(1)}, bf16[32,256]{1,0:T(8,128)(2,1)}, u32[]{:S(2)}) copy-start(bf16[32,256]{1,0:T(8,128)(2,1)} %sf_in.1) | copy-start | bytes 49156

commit v4 on v3

--- a/solution.py
+++ b/solution.py
@@ -157,6 +157,8 @@
     for d in range(1, NY):
         arrive(fb.at[:, (y + NY - d) % NY], fb_y, d - 1, at_y((y + d) % NY))
 
+    gathers = list(sent)
+    sent.clear()
     used = counts[0]
     per_z = TILE // (NY * ROWS)
     per_x = TILE // ROWS
@@ -207,7 +209,7 @@
         for e in range(per_z if shift else 1):
             there = k * per_z + e if shift else own_block * per_z + (z + 1) % per_z
             send(pa.at[there], za.at[z], sa_z, (n * per_z + e, z), at_z(there))
-    for d in range(1, NY):
+    for d in (2, 1, 3):
         there = (y + d) % NY
         send(pb.at[:, there], yb.at[d - 1], sb_y, d - 1, at_y(there))
 
@@ -273,6 +275,8 @@
 
     errors(0)
 
+    for one in gathers:
+        one.wait_send()
     for n, (i, j) in enumerate(NEAR):
         arrive(rx.at[n], t_x, n, at_near(i, j))
     total = pt[pl.ds(x * NH, NH), c].astype(F32)

time: 43.3 us -> 43.2 us (level)
  no operation moved by 1% of the time
where the time goes in v4:
time: 43.2 us; the launch traced here: 43 us
  Pallas kernels  40.3 us (93%)
  other arithmetic  1.41 us (3%)
  between operations  1.32 us (3%)
    pallas_call x1, Pallas kernels, shards(): pl.pallas_call(kernel, out_shape=own, in_specs=[anywhere] * 7, out_specs=...  40.3 us
    add x1, other arithmetic, shards(): both[1] + 0.5 * time_factors.astype(F32)  1.41 us

profile of v4, /device:TPU:1, one launch (start us, length us, event | category | flops | bytes accessed | tf_op | source)
XLA Modules:
  0.0 43.0 jit_solution(18167711120406897271)
XLA Ops:
  1.3 0.0 copy-start
  1.3 0.0 copy-start.1
  1.3 40.3 %shard_map.86 = f32[2,32,256]{2,1,0:T(8,128)} custom-call(bf16[32,256]{1,0:T(8,128)(2,1)} %sf_in.1, bf16[32,256]{1,0:T(8,128)(2,1)} %tf_in.1, bf16[8,256,256]{2,1,0:T(8,128)(2,1)} %values.1, s32[2,8]{1,0:T(2,128)} %bitcast.5, s32[1]{0:T(128)S(6)} %copy.9.counts_in, s32[96]{0:T(128)} %lags_in.1, f32[96,256]{1,0:T(8,128)} %weights_in.1), custom_call_target="tpu_custom_call" | custom-call | flops 805306368 | bytes 1048576 | tf_op jit(solution)/shard_map/pallas_call | solution.py:349
  41.6 0.0 copy-done
  41.6 0.0 copy-done.1
  41.6 1.4 %bitcast_add_fusion = (f32[32,256]{1,0:T(8,128)}, f32[32,256]{1,0:T(8,128)}) fusion(bf16[32,256]{1,0:T(8,128)(2,1)S(1)} %copy-done, f32[2,32,256]{2,1,0:T(8,128)} %shard_map.86, bf16[32,256]{1,0:T(8,128)(2,1)S(1)} %copy-done.1), kind=kLoop, calls=%fused_computation | loop fusion | flops 49152 | bytes 163840 | tf_op jit(solution)/shard_map/add | solution.py:399
Async XLA Ops:
  1.3 40.3 %copy-start = (bf16[32,256]{1,0:T(8,128)(2,1)S(1)}, bf16[32,256]{1,0:T(8,128)(2,1)}, u32[]{:S(2)}) copy-start(bf16[32,256]{1,0:T(8,128)(2,1)} %tf_in.1) | copy-start | bytes 49156
  1.3 40.3 %copy-start.1 = (bf16[32,256]{1,0:T(8,128)(2,1)S(1)}, bf16[32,256]{1,0:T(8,128)(2,1)}, u32[]{:S(2)}) copy-start(bf16[32,256]{1,0:T(8,128)(2,1)} %sf_in.1) | copy-start | bytes 49156

commit v5 on v3

--- a/solution.py
+++ b/solution.py
@@ -185,8 +185,9 @@
     def gathered(acc, places, k, piece):
         total = jnp.zeros((rows_at_once, TILE), F32)
         for m, place in enumerate(places):
-            total = total + jnp.where(place == k, acc[m, pl.ds(pl.multiple_of(piece * rows_at_once, rows_at_once), rows_at_once)], 0.0)
-        return (total * scale).astype(BF16)
+            share = jnp.where(place == k, scale, 0.0)
+            total = total + share * acc[m, pl.ds(pl.multiple_of(piece * rows_at_once, rows_at_once), rows_at_once)]
+        return total.astype(BF16)
 
     per = NY * ROWS // rows_at_once
     own_block = z // per_z

time: 43.3 us -> 43.3 us (level)
  no operation moved by 1% of the time
where the time goes in v5:
time: 43.3 us; the launch traced here: 43 us
  Pallas kernels  40.3 us (93%)
  other arithmetic  1.41 us (3%)
  between operations  1.32 us (3%)
    pallas_call x1, Pallas kernels, shards(): pl.pallas_call(kernel, out_shape=own, in_specs=[anywhere] * 7, out_specs=...  40.3 us
    add x1, other arithmetic, shards(): both[1] + 0.5 * time_factors.astype(F32)  1.41 us

profile of v5, /device:TPU:1, one launch (start us, length us, event | category | flops | bytes accessed | tf_op | source)
XLA Modules:
  0.0 43.0 jit_solution(3693158679446253406)
XLA Ops:
  1.3 0.0 copy-start
  1.3 0.0 copy-start.1
  1.3 40.3 %shard_map.86 = f32[2,32,256]{2,1,0:T(8,128)} custom-call(bf16[32,256]{1,0:T(8,128)(2,1)} %sf_in.1, bf16[32,256]{1,0:T(8,128)(2,1)} %tf_in.1, bf16[8,256,256]{2,1,0:T(8,128)(2,1)} %values.1, s32[2,8]{1,0:T(2,128)} %bitcast.5, s32[1]{0:T(128)S(6)} %copy.9.counts_in, s32[96]{0:T(128)} %lags_in.1, f32[96,256]{1,0:T(8,128)} %weights_in.1), custom_call_target="tpu_custom_call" | custom-call | flops 805306368 | bytes 1048576 | tf_op jit(solution)/shard_map/pallas_call | solution.py:346
  41.6 0.0 copy-done
  41.6 0.0 copy-done.1
  41.6 1.4 %bitcast_add_fusion = (f32[32,256]{1,0:T(8,128)}, f32[32,256]{1,0:T(8,128)}) fusion(bf16[32,256]{1,0:T(8,128)(2,1)S(1)} %copy-done, f32[2,32,256]{2,1,0:T(8,128)} %shard_map.86, bf16[32,256]{1,0:T(8,128)(2,1)S(1)} %copy-done.1), kind=kLoop, calls=%fused_computation | loop fusion | flops 49152 | bytes 163840 | tf_op jit(solution)/shard_map/add | solution.py:396
Async XLA Ops:
  1.3 40.3 %copy-start = (bf16[32,256]{1,0:T(8,128)(2,1)S(1)}, bf16[32,256]{1,0:T(8,128)(2,1)}, u32[]{:S(2)}) copy-start(bf16[32,256]{1,0:T(8,128)(2,1)} %tf_in.1) | copy-start | bytes 49156
  1.3 40.3 %copy-start.1 = (bf16[32,256]{1,0:T(8,128)(2,1)S(1)}, bf16[32,256]{1,0:T(8,128)(2,1)}, u32[]{:S(2)}) copy-start(bf16[32,256]{1,0:T(8,128)(2,1)} %sf_in.1) | copy-start | bytes 49156
